TPU v7x, 256 devices: a whole 4x4x8 slice. The times are simulated.
256 devices in a mesh: dp: 4 (over y), space: 64 (over x, z, core).
Axes of the slice: x: 4, y: 4, z: 8, core: 2. Of those that a mesh axis runs over, the one named last changes fastest.
Arguments:
- features: bfloat16 [65536, 256], P(('dp', 'space')), parts along dimension 0, may hold values from -16 to 16
- conv_weight: bfloat16 [27, 256, 256], replicated, may hold values from -0.125 to 0.125
- down_weight: bfloat16 [8, 256, 256], replicated, may hold values from -0.25 to 0.25
- grad_conv: bfloat16 [65536, 256], P(('dp', 'space')), parts along dimension 0, may hold values from -6 to 6
- grad_down: bfloat16 [32768, 256], P(('dp', 'space')), parts along dimension 0, may hold values from -6 to 6
- live_rows: int32 [256], P(('dp', 'space')), parts along dimension 0, may hold values from 128 to 256, as said below
- halo_send: int32 [256, 128], P(('dp', 'space')), parts along dimension 0, may hold values from -1 to 255, as said below
- neighbors: int32 [27, 65536], P(None, ('dp', 'space')), parts along dimension 1, may hold values from -1 to 383, as said below
- coarse_code: int32 [65536], P(('dp', 'space')), parts along dimension 0, may hold values from -1 to 1023, as said below
Outputs:
- conv_out: bfloat16 [65536, 256], P(('dp', 'space')), parts along dimension 0
- down_out: bfloat16 [32768, 256], P(('dp', 'space')), parts along dimension 0
- grad_features: bfloat16 [65536, 256], P(('dp', 'space')), parts along dimension 0
- conv_grad: float32 [108, 256, 256], P('dp', 'space'), parts along dimension 0
- down_grad: float32 [32, 256, 256], P('dp', 'space'), parts along dimension 0
There are 4 independent parts, one for each index of `dp`. A program takes and returns all parts, laid end to end along the dimension named above; an argument that names none is the same for every part. Nothing has to cross between parts.
Inputs may be any that keep to these rules, and one draw needn't show every extreme that they name: Rows 0 to live_rows[d] - 1 of device d are occupied voxels, the others are empty; in every draw one device has 256 and one has 128. `halo_send`: entry p * 2 + s of device d's list is the occupied local row that d sends to device p in slot s, or -1 for an empty slot. `neighbors`: tap k = 9a + 3b + c stands for the offset (a - 1, b - 1, c - 1). A value below 256 is an occupied row of the same device; a value 256 + p * 2 + s is slot s of what device p sends to this device, never an empty slot; -1 means no neighbour. Tap 13 is the row itself; empty rows have -1 at every tap. `coarse_code`: -1 for empty rows; else (p * 2 + j) * 8 + o: coarse slot j toward device p, child offset o = 4a + 2b + c in the 2x2x2 cell; no two rows of a device share a value.
All inputs are finite; a program needn't handle non-finite values.
Results may differ from a plain program's by a relative error of at most 0.0055.
Values may be sent and summed in bfloat16 or wider, within the bound.
A program may use at most 128 MiB of HBM per device.

v0:
```python
import jax
import jax.numpy as jnp
from jax import lax
from jax.sharding import PartitionSpec as P


def conv_forward(extended, conv_weight, tap_rows, channels):

    def add_tap(running, tap_item):
        weight_tap, rows_at = tap_item
        picked = jnp.take(extended, rows_at, axis=0)
        return (running + jnp.dot(picked, weight_tap, preferred_element_type=jnp.float32), None)

    start_sum = jnp.zeros((tap_rows.shape[1], channels), jnp.float32)
    return lax.scan(add_tap, start_sum, (conv_weight, tap_rows))[0]


def per_device(
    features,
    conv_weight,
    down_weight,
    grad_conv,
    grad_down,
    live_rows,
    halo_send,
    neighbors,
    coarse_code,
):
    row_count, channels = features.shape
    peer_count = lax.axis_size("space")
    halo_size = halo_send.shape[1]
    slot_size = halo_size // peer_count
    coarse_count = grad_down.shape[0]
    coarse_slot = coarse_count // peer_count
    grad_scale = 256.0 / (row_count * peer_count)
    occupied = jnp.arange(row_count, dtype=jnp.int32) < live_rows[0]
    zero_row = jnp.zeros((1, channels), jnp.bfloat16)
    padded = jnp.concatenate([features, zero_row], axis=0)
    send_rows = jnp.where(halo_send[0] >= 0, halo_send[0], row_count)
    outgoing = jnp.take(padded, send_rows, axis=0).reshape(peer_count, slot_size, channels)
    incoming = lax.all_to_all(outgoing, "space", split_axis=0, concat_axis=0, tiled=True).reshape(
        halo_size, channels
    )
    extended = jnp.concatenate([features, incoming, zero_row], axis=0)
    ext_count = row_count + halo_size + 1
    tap_rows = jnp.where(neighbors < 0, ext_count - 1, neighbors)
    summed = conv_forward(extended, conv_weight, tap_rows, channels)
    conv_out = jnp.where(occupied[:, None], summed, 0.0).astype(jnp.bfloat16)
    child_pos = jnp.where(coarse_code >= 0, coarse_code, coarse_count * 8)
    child_row = (
        jnp.full((coarse_count * 8,), row_count, jnp.int32)
        .at[child_pos]
        .set(jnp.arange(row_count, dtype=jnp.int32), mode="drop")
    )
    conv_padded = jnp.concatenate([conv_out, zero_row], axis=0)
    children = jnp.take(conv_padded, child_row, axis=0).reshape(coarse_count, 8 * channels)
    down_flat = down_weight.reshape(8 * channels, channels)
    coarse_part = jnp.dot(children, down_flat, preferred_element_type=jnp.float32).astype(
        jnp.bfloat16
    )
    down_out = lax.all_to_all(
        coarse_part.reshape(peer_count, coarse_slot, channels),
        "space",
        split_axis=0,
        concat_axis=0,
        tiled=True,
    ).reshape(coarse_count, channels)
    coarse_back = lax.all_to_all(
        grad_down.reshape(peer_count, coarse_slot, channels),
        "space",
        split_axis=0,
        concat_axis=0,
        tiled=True,
    ).reshape(coarse_count, channels)
    down_term = lax.dot_general(
        children, coarse_back, (((0,), (0,)), ((), ())), preferred_element_type=jnp.float32
    )
    down_term = (down_term * grad_scale).reshape(8, channels, channels)
    spread = lax.dot_general(
        coarse_back, down_flat, (((1,), (1,)), ((), ())), preferred_element_type=jnp.float32
    )
    spread = jnp.concatenate(
        [spread.reshape(coarse_count * 8, channels), jnp.zeros((1, channels), jnp.float32)], axis=0
    )
    from_down = jnp.take(spread, child_pos, axis=0)
    total_grad = jnp.where(
        occupied[:, None], grad_conv.astype(jnp.float32) + from_down, 0.0
    ).astype(jnp.bfloat16)

    def back_tap(carried, tap_item):
        weight_tap, rows_at = tap_item
        picked = jnp.take(extended, rows_at, axis=0)
        tap_grad = lax.dot_general(
            picked, total_grad, (((0,), (0,)), ((), ())), preferred_element_type=jnp.float32
        )
        pulled = lax.dot_general(
            total_grad, weight_tap, (((1,), (1,)), ((), ())), preferred_element_type=jnp.float32
        )
        return (
            carried + jax.ops.segment_sum(pulled, rows_at, num_segments=ext_count),
            tap_grad * grad_scale,
        )

    ext_grad = jnp.zeros((ext_count, channels), jnp.float32)
    pieces = []
    for group_start in range(0, 27, 9):
        ext_grad, tap_grads = lax.scan(
            back_tap,
            ext_grad,
            (conv_weight[group_start : group_start + 9], tap_rows[group_start : group_start + 9]),
        )
        pieces.append(tap_grads)
    conv_grad = jnp.concatenate(pieces, axis=0)
    conv_grad, down_grad = (
        lax.psum_scatter(conv_grad, "space", scatter_dimension=1, tiled=True),
        lax.psum_scatter(down_term, "space", scatter_dimension=1, tiled=True),
    )
    halo_grad = ext_grad[row_count : row_count + halo_size].reshape(peer_count, slot_size, channels)
    returned = (
        lax.all_to_all(
            halo_grad.astype(jnp.bfloat16), "space", split_axis=0, concat_axis=0, tiled=True
        )
        .astype(halo_grad.dtype)
        .reshape(halo_size, channels)
    )
    back_rows = jax.ops.segment_sum(returned, send_rows, num_segments=row_count + 1)[:row_count]
    grad_features = (ext_grad[:row_count] + back_rows).astype(jnp.bfloat16)
    return (conv_out, down_out, grad_features, conv_grad, down_grad)


def solution(mesh):
    placed = (
        P(("dp", "space"), None),
        P(),
        P(),
        P(("dp", "space"), None),
        P(("dp", "space"), None),
        P(("dp", "space")),
        P(("dp", "space"), None),
        P(None, ("dp", "space")),
        P(("dp", "space")),
    )
    return jax.shard_map(
        per_device,
        mesh=mesh,
        in_specs=placed,
        out_specs=(
            P(("dp", "space"), None),
            P(("dp", "space"), None),
            P(("dp", "space"), None),
            P("dp", "space", None),
            P("dp", "space", None),
        ),
        check_vma=False,
    )
```

profile of v0, /device:TPU:16, one launch (start us, length us, event | category | flops | bytes accessed | tf_op | source)
XLA Modules:
  0.0 584.6 jit_solution(6059513837711633803)
XLA Ops:
  8.8 11.9 %all-to-all-start.2 = ((bf16[64,2,256]{2,1,0:T(2,128)(2,1)}), bf16[64,2,256]{2,1,0:T(2,128)(2,1)S(1)}, u32[]{:S(2)}, u32[]{:S(2)}) async-start(bf16[64,2,256]{2,1,0:T(2,128)(2,1)} %reshape.136), calls=%async_computation.2 | async-start | bytes 131072 | tf_op jit(solution)/shard_map/all_to_all | solution.py:68
  29.4 3.8 fusion.43
  34.3 10.3 %all-to-all-start = ((bf16[64,2,256]{2,1,0:T(2,128)(2,1)}), bf16[64,2,256]{2,1,0:T(2,128)(2,1)S(1)}, u32[]{:S(2)}, u32[]{:S(2)}) async-start(bf16[64,2,256]{2,1,0:T(2,128)(2,1)} %broadcast_select_fusion.1), calls=%async_computation | async-start | bytes 131072 | tf_op jit(solution)/shard_map/all_to_all | solution.py:41
  48.8 5.5 all-to-all-done
  56.4 52.2 %while.47 = (s32[]{:T(128)}, f32[385,256]{1,0:T(8,128)S(1)}, f32[9,256,256]{2,1,0:T(8,128)}, s32[9,256]{1,0:T(8,128)S(1)}, bf16[9,256,256]{2,1,0:T(8,128)(2,1)},...) while((s32[]{:T(128)}, f32[385,256]{1,0:T(8,128)S(1)}, ...), condition=%wide.region_5.7_spmd, body=%wide.region_3.6_spmd.sunk | while | flops 67308800 | bytes 2635353 | solution.py:107
  71.4 2.3 scatter_fusion
  88.9 2.3 scatter_fusion
  110.2 52.1 %while.48 = (s32[]{:T(128)}, f32[385,256]{1,0:T(8,128)S(1)}, f32[9,256,256]{2,1,0:T(8,128)}, s32[9,256]{1,0:T(8,128)S(1)}, bf16[9,256,256]{2,1,0:T(8,128)(2,1)},...) while((s32[]{:T(128)}, f32[385,256]{1,0:T(8,128)S(1)}, ...), condition=%wide.region_8.10_spmd, body=%wide.region_6.9_spmd.sunk | while | flops 67308800 | bytes 2635353 | solution.py:107
  119.5 2.3 scatter_fusion.1
  154.2 2.3 scatter_fusion.1
  162.3 65.4 %while.50 = (s32[]{:T(128)}, f32[256,256]{1,0:T(8,128)S(1)}, s32[27,256]{1,0:T(8,128)S(1)}, bf16[385,256]{1,0:T(8,128)(2,1)S(1)}, bf16[27,256,256]{2,1,0:T(8,128)(2,1)}, /*index=5*/s32[]{:T(128)}, s32[]{:T(128)}) while((s32[]{:T(128)}, f32[256,256]{1,0:T(8,128)S(1)}, s32[27,256]{1,0:T(8,128)S(1)}, bf16[385,256]{1,0:T(8,128)(2,1)S(1)}, ...), condition=%wide.region_1.3_spmd.clone, body=%wide.region_0.2_spmd.clone.sunk | while | flops 33754368 | bytes 1060955 | solution.py:15
  227.8 3.9 gather_fusion.5
  232.7 2.5 copy.30
  237.2 52.2 %while.49 = (s32[]{:T(128)}, f32[385,256]{1,0:T(8,128)S(1)}, f32[9,256,256]{2,1,0:T(8,128)}, s32[9,256]{1,0:T(8,128)S(1)}, bf16[9,256,256]{2,1,0:T(8,128)(2,1)},...) while((s32[]{:T(128)}, f32[385,256]{1,0:T(8,128)S(1)}, ...), condition=%wide.region_11.13_spmd, body=%wide.region_9.12_spmd.sunk | while | flops 67308800 | bytes 2635353 | solution.py:107
  258.1 2.3 scatter_fusion.2
  263.9 2.3 scatter_fusion.2
  281.4 2.3 scatter_fusion.2
  289.5 5.3 pad_maximum_fusion
  295.5 4.6 all-to-all-start.3
  301.2 8.7 %all-to-all-done.3 = bf16[64,2,256]{2,1,0:T(2,128)(2,1)S(1)} async-done(((bf16[64,2,256]{2,1,0:T(2,128)(2,1)}), bf16[64,2,256]{2,1,0:T(2,128)(2,1)S(1)}, u32[]{:S(2)}, u32[]{:S(2)}) %all-to-all-start.3) | async-done | bytes 65568 | tf_op jit(solution)/shard_map/all_to_all | solution.py:120
  309.8 4.6 all-to-all-start.1
  317.0 7.5 %all-to-all-done.1 = bf16[64,2,256]{2,1,0:T(2,128)(2,1)S(1)} async-done(((bf16[64,2,256]{2,1,0:T(2,128)(2,1)}), bf16[64,2,256]{2,1,0:T(2,128)(2,1)S(1)}, u32[]{:S(2)}, u32[]{:S(2)}) %all-to-all-start.1) | async-done | bytes 65568 | tf_op jit(solution)/shard_map/all_to_all | solution.py:61
  325.9 45.9 %reduce-scatter.3.cloned.1.call-done = f32[8,4,256]{2,0,1:T(8,128)} async-done(((f32[8,256,256]{2,0,1:T(8,128)}), f32[8,4,256]{2,0,1:T(8,128)}) %reduce-scatter.3.cloned.1.call-update) | async-done | bytes 32784 | tf_op jit(solution)/shard_map/reduce_scatter | solution.py:116
  373.1 203.0 %all-reduce.6.cloned.1.call-done = f32[27,256,256]{2,1,0:T(8,128)} async-done(((f32[27,256,256]{2,1,0:T(8,128)}), f32[27,256,256]{2,1,0:T(8,128)}) %all-reduce.6.cloned.1.call-update) | async-done | bytes 7077904
  (466 shorter events, 231.9 us)
Async XLA Ops:
  7.2 37.7 %copy-start = (bf16[8,256,256]{2,1,0:T(8,128)(2,1)S(1)}, bf16[8,256,256]{2,1,0:T(8,128)(2,1)}, u32[]{:S(2)}) copy-start(bf16[8,256,256]{2,1,0:T(8,128)(2,1)} %param.21) | copy-start | bytes 3145732
  8.8 25.5 %all-to-all-start.2 = ((bf16[64,2,256]{2,1,0:T(2,128)(2,1)}), bf16[64,2,256]{2,1,0:T(2,128)(2,1)S(1)}, u32[]{:S(2)}, u32[]{:S(2)}) async-start(bf16[64,2,256]{2,1,0:T(2,128)(2,1)} %reshape.136), calls=%async_computation.2 | async-start | bytes 131072 | tf_op jit(solution)/shard_map/all_to_all | solution.py:68
  34.3 20.1 %all-to-all-start = ((bf16[64,2,256]{2,1,0:T(2,128)(2,1)}), bf16[64,2,256]{2,1,0:T(2,128)(2,1)S(1)}, u32[]{:S(2)}, u32[]{:S(2)}) async-start(bf16[64,2,256]{2,1,0:T(2,128)(2,1)} %broadcast_select_fusion.1), calls=%async_computation | async-start | bytes 131072 | tf_op jit(solution)/shard_map/all_to_all | solution.py:41
  44.6 327.1 %reduce-scatter.3.cloned.1.call-start = ((), (), s32[]{:S(2)}) async-start(), calls=%async_computation.5 | async-start | bytes 2129920 | tf_op jit(solution)/shard_map/reduce_scatter | solution.py:116
  46.5 7.9 %copy-start.1 = (bf16[256,256]{1,0:T(8,128)(2,1)S(1)}, bf16[256,256]{1,0:T(8,128)(2,1)}, u32[]{:S(2)}) copy-start(bf16[256,256]{1,0:T(8,128)(2,1)} %param.19) | copy-start | bytes 393220
  46.5 8.0 %copy-start.3 = (bf16[256,256]{1,0:T(8,128)(2,1)S(1)}, bf16[256,256]{1,0:T(8,128)(2,1)}, u32[]{:S(2)}) copy-start(bf16[256,256]{1,0:T(8,128)(2,1)} %param.22) | copy-start | bytes 393220
  227.8 4.0 copy-start.2
  235.2 340.9 %all-reduce.6.cloned.1.call-start = ((), (), s32[]{:S(2)}) async-start(), calls=%async_computation.6 | async-start | bytes 14155776
  294.8 19.7 %copy-start.4 = (u32[256]{0:T(256)S(1)}, u32[256]{0:T(256)}, u32[]{:S(2)}) copy-start(u32[256]{0:T(256)} %constant.130) | copy-start | bytes 3076
  295.5 14.3 %all-to-all-start.3 = ((bf16[64,2,256]{2,1,0:T(2,128)(2,1)}), bf16[64,2,256]{2,1,0:T(2,128)(2,1)S(1)}, u32[]{:S(2)}, u32[]{:S(2)}) async-start(bf16[64,2,256]{2,1,0:T(2,128)(2,1)} %convert_element_type.24), calls=%async_computation.3 | async-start | bytes 131072 | tf_op jit(solution)/shard_map/all_to_all | solution.py:120
  309.8 14.7 %all-to-all-start.1 = ((bf16[64,2,256]{2,1,0:T(2,128)(2,1)}), bf16[64,2,256]{2,1,0:T(2,128)(2,1)S(1)}, u32[]{:S(2)}, u32[]{:S(2)}) async-start(bf16[64,2,256]{2,1,0:T(2,128)(2,1)} %reshape.134), calls=%async_computation.1 | async-start | bytes 131072 | tf_op jit(solution)/shard_map/all_to_all | solution.py:61
Sparse Core Ops, SparseCore 0:
  235.4 136.3 reduce-scatter.2
  375.8 200.3 all-reduce.5
where the time goes:
time: 586 us; the launch traced here: 585 us
  waiting for transfers between devices  271 us (46%)
  local copies, waits for them, and re-layouts  96.7 us (17%)
  matrix products  91.3 us (16%)
  other arithmetic  75.1 us (13%)
  starting transfers between devices  32 us (5%)
  between operations  15.6 us (3%)
    unnamed x3, waiting for transfers between devices  203 us
    scatter-add x27, other arithmetic, back_tap(): jax.ops.segment_sum(pulled, rows_at, num_segments=ext_count)  61.5 us
    reduce_scatter x1, waiting for transfers between devices, per_device(): lax.psum_scatter(down_term, 'space', scatter_dimension=1, tiled=True)  45.9 us
    dot_general x27, matrix products, add_tap(): jnp.dot(picked, weight_tap, preferred_element_type=jnp.float32)  32 us
    gather x27, local copies, waits for them, and re-layouts, back_tap(): picked = jnp.take(extended, rows_at, axis=0)  31.1 us
    gather x27, local copies, waits for them, and re-layouts, add_tap(): picked = jnp.take(extended, rows_at, axis=0)  31.1 us
    dot_general x27, matrix products, back_tap(): lax.dot_general(total_grad, weight_tap, (((1,), (1,)), ((), ())), preferr...  30.2 us
    dot_general x27, matrix products, back_tap(): lax.dot_general(picked, total_grad, (((0,), (0,)), ((), ())), preferred_e...  27.8 us
  transfers between devices with their start and end apart: 6, of which 5 were waited for; matrix products, arithmetic and copies ran while one was open for 14% of the time, Pallas kernels for 0%

commit v1 on v0

v1 whole, which is shorter than its diff:
```python
import jax
import jax.numpy as jnp
from jax import lax
from jax.experimental import pallas as pl
from jax.experimental.pallas import tpu as pltpu
from jax.sharding import PartitionSpec as P

MESH = pl.DeviceIdType.MESH
BF16, F32, I32 = jnp.bfloat16, jnp.float32, jnp.int32
NX, NZ, PEERS = 4, 8, 64
TAPS, GROUPS = 27, 9
CHUNKS = ((0, 4), (4, 7), (7, 9))


def mm(a, b):
    return jnp.dot(a, b, preferred_element_type=F32)


def mm_nt(a, b):
    return lax.dot_general(a, b, (((1,), (1,)), ((), ())), preferred_element_type=F32)


def mm_tn(a, b):
    return lax.dot_general(a, b, (((0,), (0,)), ((), ())), preferred_element_type=F32)


def onehot(mask):
    return jnp.where(mask, 1.0, 0.0).astype(BF16)


def iota(shape, dim):
    return lax.broadcasted_iota(I32, shape, dim)


def slot_row(q, kind, half):
    return 8 * (q // 2) + 2 * (2 * kind + q % 2) + half


def pack(first, second):
    row, q = iota((512, 128), 0), iota((512, 128), 1)
    total = jnp.zeros((512, 128), F32)
    for kind, rows in ((0, first), (1, second)):
        for half in range(2):
            place = onehot(row == slot_row(q, kind, half))
            total += mm(place, rows[:, half * 128 : half * 128 + 128])
    return total.reshape(PEERS, 8, 128).astype(BF16)


def unpack(slots, kind):
    q, row = iota((128, 512), 0), iota((128, 512), 1)
    flat = slots.astype(F32).reshape(512, 128).astype(BF16)
    return jnp.concatenate(
        [mm(onehot(row == slot_row(q, kind, half)), flat) for half in range(2)], axis=1
    )


def interleave(terms):
    a = [term.reshape(32, 8, 256) for term in terms]
    r = [pltpu.roll(value, 4, 1) for value in a]
    low = iota((32, 8, 256), 1) < 4
    first = jnp.concatenate(
        [jnp.where(low, a[0], r[1]), jnp.where(low, a[2], r[3])], axis=1
    )
    second = jnp.concatenate(
        [jnp.where(low, r[0], a[1]), jnp.where(low, r[2], a[3])], axis=1
    )
    return first.astype(BF16), second.astype(BF16)


def kernel(
    feat_ref,
    w_hbm,
    wd_hbm,
    gconv_ref,
    gdown_ref,
    live_ref,
    send_ref,
    nbr_ref,
    code_ref,
    conv_ref,
    down_ref,
    gfeat_ref,
    wg_ref,
    dg_ref,
    w_ref,
    wd_ref,
    oht,
    picked,
    cbo,
    total_ref,
    acc,
    ext_grad,
    a1_src,
    a1_dst,
    a2_src,
    a2_dst,
    part,
    got0,
    got1,
    got2,
    summed,
    got3,
    w_sem,
    a_ss,
    a_rs,
    s0,
    r0,
    s1,
    r1,
    s2,
    r2,
    s3,
    r3,
):
    me = lax.axis_index("space")
    x, z, core = me // 16, (me // 2) % NZ, me % 2
    x1, x2, x3 = x + 1 - 2 * (x % 2), (x + 2) % NX, 3 - x

    def device(xx, zz, cc):
        return {"space": (xx * NZ + zz) * 2 + cc}

    barrier = pltpu.get_barrier_semaphore()

    def greet(i, carry):
        pl.semaphore_signal(
            barrier, inc=1, device_id={"space": (me + i) % PEERS}, device_id_type=MESH
        )
        return carry

    lax.fori_loop(1, PEERS, greet, 0)
    w_copy = pltpu.make_async_copy(w_hbm, w_ref, w_sem.at[0])
    wd_copy = pltpu.make_async_copy(wd_hbm, wd_ref, w_sem.at[1])
    w_copy.start()
    wd_copy.start()

    def exchange(src, dst, which):
        def send(i, carry):
            peer = (me + i) % PEERS
            pltpu.make_async_remote_copy(
                src_ref=src.at[peer],
                dst_ref=dst.at[me],
                send_sem=a_ss.at[which],
                recv_sem=a_rs.at[which],
                device_id={"space": peer},
                device_id_type=MESH,
            ).start()
            return carry

        pltpu.make_async_copy(src.at[me], dst.at[me], a_rs.at[which]).start()
        lax.fori_loop(1, PEERS, send, 0)

    def exchange_wait(src, dst, which):
        pltpu.make_async_copy(src, dst, a_rs.at[which]).wait()

    def exchange_sent(src, dst, which):
        rest = pl.ds(0, PEERS - 1)
        pltpu.make_async_copy(src.at[rest], dst.at[rest], a_ss.at[which]).wait()

    feat = feat_ref[...]
    send_hot = onehot(iota((256, 128), 0) == send_ref[...])
    a1_src[...] = pack(mm_tn(send_hot, feat).astype(BF16), gdown_ref[...])
    pl.semaphore_wait(barrier, PEERS - 1)
    exchange(a1_src, a1_dst, 0)

    feat_t = feat.astype(F32).T.astype(BF16)
    acc[...] = jnp.zeros((256, 256), F32)
    picked[TAPS] = jnp.zeros((256, 256), BF16)
    oht[TAPS] = jnp.zeros((384, 256), BF16)
    w_copy.wait()

    def local_tap(k, carry):
        hot = onehot(iota((384, 256), 0) == nbr_ref[pl.ds(k, 1), :])
        oht[k] = hot
        own = mm(feat_t, hot[:256]).astype(BF16)
        picked[k] = own
        acc[...] += mm_tn(own, w_ref[k])
        return carry

    lax.fori_loop(0, TAPS, local_tap, 0)
    wd_copy.wait()

    exchange_wait(a1_src, a1_dst, 0)
    arrived = a1_dst[...]
    halo_t = unpack(arrived, 0).T.astype(BF16)
    coarse_back = unpack(arrived, 1).astype(BF16)
    code_row = code_ref[...]
    code_col = jnp.broadcast_to(code_row.astype(F32), (8, 256)).T[:, :1].astype(I32)
    from_down = jnp.zeros((256, 256), F32)
    for o in range(8):
        rows = mm(onehot(code_col == 8 * iota((256, 128), 1) + o), coarse_back).astype(BF16)
        cbo[o] = rows
        from_down += mm_nt(rows, wd_ref[o])
    occupied = iota((256, 256), 0) < live_ref[...]
    total = jnp.where(occupied, gconv_ref[...].astype(F32) + from_down, 0.0).astype(BF16)
    total_ref[...] = total

    def remote(src, dst, ss, rs, to):
        return pltpu.make_async_remote_copy(
            src_ref=src, dst_ref=dst, send_sem=ss, recv_sem=rs, device_id=to, device_id_type=MESH
        )

    def core_copy(g):
        return remote(part.at[1 - core, g], got0.at[g], s0.at[g], r0.at[g], device(x, z, 1 - core))

    za, zb = pl.ds(0, 4), pl.ds(4, 4)

    def x_copies(g):
        mine = part.at[core, g]
        there = got1.at[g]
        return [
            remote(mine.at[src, zs], there.at[slot, zs], s1.at[g, n], r1.at[g, n], device(to, z, core))
            for n, (src, slot, zs, to) in enumerate(
                ((x1, 0, za, x1), (x2, 1, za, x1), (x3, 0, zb, x3), (x2, 1, zb, x3))
            )
        ]

    def x_last(g):
        mine = part.at[core, g]
        there = got2.at[g]
        return [
            remote(mine.at[to, zs], there.at[zs], s2.at[g, n], r2.at[g, n], device(to, z, core))
            for n, (zs, to) in enumerate(((za, x3), (zb, x1)))
        ]

    def z_copies(c):
        span = pl.ds(CHUNKS[c][0], CHUNKS[c][1] - CHUNKS[c][0])
        out = []
        for i in range(1, NZ):
            to = (z + i) % NZ
            out.append(
                remote(
                    summed.at[span, to], got3.at[z, span], s3.at[c, i], r3.at[c, i], device(x, to, core)
                )
            )
        return out

    def give(g, terms):
        first, second = interleave(terms)
        part[0, g] = first.reshape(NX, NZ, 16, 256)
        part[1, g] = second.reshape(NX, NZ, 16, 256)
        core_copy(g).start()

    def conv_group(g):
        terms = []
        for t in range(4):
            k = 4 * g + t
            whole = picked[k] + mm(halo_t, oht[k, 256:384]).astype(BF16)
            terms.append(mm(whole, total_ref[...]))
        give(g, terms)

    def add(g, xx, zs, other):
        here = part[core, g, xx, zs].astype(F32) + other.astype(F32)
        part[core, g, xx, zs] = here.astype(BF16)

    def step1(g):
        core_copy(g).wait_recv()
        for xx in range(NX):
            part[core, g, xx] = (part[core, g, xx].astype(F32) + got0[g, xx].astype(F32)).astype(BF16)
        for copy in x_copies(g):
            copy.start()

    def step2(g):
        for copy in x_copies(g):
            copy.wait_recv()
        add(g, x3, za, got1[g, 1, za])
        add(g, x1, zb, got1[g, 1, zb])
        for copy in x_last(g):
            copy.start()
        add(g, x, za, got1[g, 0, za])
        add(g, x, zb, got1[g, 0, zb])

    def step3(g):
        for copy in x_last(g):
            copy.wait_recv()
        summed[g] = (part[core, g, x].astype(F32) + got2[g].astype(F32)).astype(BF16)

    def step4(c):
        for copy in z_copies(c):
            copy.start()

    def final(c):
        for copy in z_copies(c):
            copy.wait_recv()
        for g in range(*CHUNKS[c]):
            value = summed[g, z].astype(F32)
            for i in range(1, NZ):
                value += got3[(z + i) % NZ, g].astype(F32)
            value = (value * (1.0 / 64.0)).reshape(4, 4, 256)
            if g < 6:
                wg_ref[4 * g : 4 * g + 4] = value
            elif g == 6:
                wg_ref[24:27] = value[:3]
            else:
                dg_ref[4 * g - 28 : 4 * g - 24] = value

    def forward(lo, hi):
        def tap(k, carry):
            rows = mm(halo_t, oht[k, 256:384]).astype(BF16)
            acc[...] += mm_tn(rows, w_ref[k])
            return carry

        lax.fori_loop(lo, hi, tap, 0)

    def backward(lo, hi):
        def tap(k, carry):
            pulled = mm_nt(total_ref[...], w_ref[k]).astype(BF16)
            ext_grad[...] += mm(oht[k], pulled)
            return carry

        lax.fori_loop(lo, hi, tap, 0)

    conv_group(0)
    conv_group(1)
    step1(0)
    conv_group(2)
    step1(1)
    conv_group(3)
    step1(2)
    step2(0)
    conv_group(4)
    step1(3)
    step2(1)
    step3(0)
    conv_group(5)
    step1(4)
    step2(2)
    step3(1)
    conv_group(6)
    step1(5)
    step2(3)
    step3(2)
    forward(0, 14)
    step1(6)
    step2(4)
    step3(3)
    step4(0)
    forward(14, 27)
    conv_out = jnp.where(occupied, acc[...], 0.0).astype(BF16)
    conv_ref[...] = conv_out
    conv_t = conv_out.astype(F32).T.astype(BF16)
    give(7, [mm(conv_t, cbo[o]) for o in range(4)])
    step2(5)
    step3(4)
    give(8, [mm(conv_t, cbo[o]) for o in range(4, 8)])
    step1(7)
    step2(6)
    step3(5)
    coarse_part = jnp.zeros((128, 256), F32)
    for o in range(8):
        hot = onehot(code_row == 8 * iota((128, 256), 0) + o)
        coarse_part += mm(mm(hot, conv_out).astype(BF16), wd_ref[o])
    step1(8)
    step2(7)
    step3(6)
    step4(1)
    ext_grad[...] = jnp.zeros((384, 256), F32)
    backward(0, 14)
    step2(8)
    step3(7)
    backward(14, 27)
    a2_src[...] = pack(coarse_part.astype(BF16), ext_grad[256:384].astype(BF16))
    exchange(a2_src, a2_dst, 1)
    step3(8)
    step4(2)
    final(0)
    final(1)
    exchange_wait(a2_src, a2_dst, 1)
    arrived = a2_dst[...]
    down_ref[...] = unpack(arrived, 0).astype(BF16)
    returned = unpack(arrived, 1).astype(BF16)
    gfeat_ref[...] = (ext_grad[:256] + mm(send_hot, returned)).astype(BF16)
    final(2)
    exchange_sent(a1_src, a1_dst, 0)
    exchange_sent(a2_src, a2_dst, 1)
    for g in range(GROUPS):
        core_copy(g).wait_send()
        for copy in x_copies(g) + x_last(g):
            copy.wait_send()
    for c in range(len(CHUNKS)):
        for copy in z_copies(c):
            copy.wait_send()


def per_device(features, conv_weight, down_weight, grad_conv, grad_down, live_rows, halo_send, neighbors, coarse_code):
    vmem = pl.BlockSpec(memory_space=pltpu.VMEM)
    hbm = pl.BlockSpec(memory_space=pl.ANY)
    dma = pltpu.SemaphoreType.DMA
    return pl.pallas_call(
        kernel,
        out_shape=(
            jax.ShapeDtypeStruct((256, 256), BF16),
            jax.ShapeDtypeStruct((128, 256), BF16),
            jax.ShapeDtypeStruct((256, 256), BF16),
            jax.ShapeDtypeStruct((27, 4, 256), F32),
            jax.ShapeDtypeStruct((8, 4, 256), F32),
        ),
        in_specs=[vmem, hbm, hbm, vmem, vmem, vmem, vmem, vmem, vmem],
        out_specs=[vmem] * 5,
        scratch_shapes=[
            pltpu.VMEM((27, 256, 256), BF16),
            pltpu.VMEM((8, 256, 256), BF16),
            pltpu.VMEM((28, 384, 256), BF16),
            pltpu.VMEM((28, 256, 256), BF16),
            pltpu.VMEM((8, 256, 256), BF16),
            pltpu.VMEM((256, 256), BF16),
            pltpu.VMEM((256, 256), F32),
            pltpu.VMEM((384, 256), F32),
            pltpu.VMEM((PEERS, 8, 128), BF16),
            pltpu.VMEM((PEERS, 8, 128), BF16),
            pltpu.VMEM((PEERS, 8, 128), BF16),
            pltpu.VMEM((PEERS, 8, 128), BF16),
            pltpu.VMEM((2, GROUPS, NX, NZ, 16, 256), BF16),
            pltpu.VMEM((GROUPS, NX, NZ, 16, 256), BF16),
            pltpu.VMEM((GROUPS, 2, NZ, 16, 256), BF16),
            pltpu.VMEM((GROUPS, NZ, 16, 256), BF16),
            pltpu.VMEM((GROUPS, NZ, 16, 256), BF16),
            pltpu.VMEM((NZ, GROUPS, 16, 256), BF16),
            dma((2,)),
            dma((2,)),
            dma((2,)),
            dma((GROUPS,)),
            dma((GROUPS,)),
            dma((GROUPS, 4)),
            dma((GROUPS, 4)),
            dma((GROUPS, 2)),
            dma((GROUPS, 2)),
            dma((3, NZ)),
            dma((3, NZ)),
        ],
        compiler_params=pltpu.CompilerParams(
            collective_id=0, has_side_effects=True, vmem_limit_bytes=56 * 2**20
        ),
        cost_estimate=pl.CostEstimate(flops=7 * 10**9, bytes_accessed=6 * 10**6, transcendentals=0),
    )(
        features,
        conv_weight,
        down_weight,
        grad_conv,
        grad_down,
        live_rows.reshape(1, 1),
        halo_send,
        neighbors,
        coarse_code.reshape(1, 256),
    )


def solution(mesh):
    rows = P(("dp", "space"), None)
    return jax.shard_map(
        per_device,
        mesh=mesh,
        in_specs=(rows, P(), P(), rows, rows, P(("dp", "space")), rows, P(None, ("dp", "space")), P(("dp", "space"))),
        out_specs=(rows, rows, rows, P("dp", "space", None), P("dp", "space", None)),
        check_vma=False,
    )
```

time: 586 us -> 91 us (0.16)
  waiting for transfers between devices: 271 us -> 0 us
  matrix products: 91.3 us -> 0 us
  local copies, waits for them, and re-layouts: 96.7 us -> 7.53 us
  Pallas kernels: 0 us -> 81.7 us
  other arithmetic: 75.1 us -> 0 us
  starting transfers between devices: 32 us -> 0 us
  between operations: 15.6 us -> 1.29 us
    unnamed x3 -> x0, waiting for transfers between devices: 203 us -> none
    dot_general x84 -> x0, matrix products: 91.3 us -> none  [the longest x27 32 us: add_tap(): jnp.dot(picked, weight_tap, preferred_element_type=jnp.float32)]
    pallas_call x0 -> x1, Pallas kernels: none -> 81.7 us  [per_device(): pl.pallas_call(kernel, out_shape=(jax.ShapeDtypeStruct((256, 256), BF16),...]
    gather x59 -> x0, local copies, waits for them, and re-layouts: 68.4 us -> none  [the longest x27 31.1 us: back_tap(): picked = jnp.take(extended, rows_at, axis=0)]
    scatter-add x28 -> x0, other arithmetic: 62.8 us -> none  [the longest x27 61.5 us: back_tap(): jax.ops.segment_sum(pulled, rows_at, num_segments=ext_count)]
    reduce_scatter x1 -> x0, waiting for transfers between devices: 45.9 us -> none  [per_device(): lax.psum_scatter(down_term, 'space', scatter_dimension=1, tiled=True)]
    all_to_all x4 -> x0, starting transfers between devices: 31.5 us -> none  [the longest x1 11.9 us: per_device(): lax.all_to_all(grad_down.reshape(peer_count, coarse_slot, channels), 'spa...]
    all_to_all x4 -> x0, waiting for transfers between devices: 21.7 us -> none  [the longest x1 8.67 us: per_device(): lax.all_to_all(halo_grad.astype(jnp.bfloat16), 'space', split_axis=0, con...]
  transfers between devices with their start and end apart: 6 -> 0, of which waited for: 5 -> 0; matrix products, arithmetic and copies ran while one was open for 14% -> 0% of each run, Pallas kernels for 0% -> 0%
where the time goes in v1:
time: 91 us; the launch traced here: 90.5 us
  Pallas kernels  81.7 us (90%)
  local copies, waits for them, and re-layouts  7.53 us (8%)
  between operations  1.29 us (1%)
    pallas_call x1, Pallas kernels, per_device(): pl.pallas_call(kernel, out_shape=(jax.ShapeDtypeStruct((256, 256), BF16),...  81.7 us
    unnamed x5, local copies, waits for them, and re-layouts  7.53 us

profile of v1, /device:TPU:16, one launch (start us, length us, event | category | flops | bytes accessed | tf_op | source)
XLA Modules:
  0.0 90.5 jit_solution(17933022239547515962)
XLA Ops:
  1.3 81.7 %shard_map.128 = (bf16[256,256]{1,0:T(8,128)(2,1)}, bf16[128,256]{1,0:T(8,128)(2,1)}, bf16[256,256]{1,0:T(8,128)(2,1)}, f32[27,4,256]{2,1,0:T(4,128)}, f32[8,4,256]{2,1,0:T(4,128)}) custom-call(bf16[256,256]{1,0:T(8,128)(2,1)} %feat_ref.1, bf16[27,256,256]{2,1,0:T(8,128)(2,1)} %w_hbm.1, bf16[8,256,256]{2,1,0:T(8,128)(2,1)} %wd_hbm.1, ...), custom_call_target="tpu_custom_call" | custom-call | flops 7000000000 | bytes 6000000 | tf_op jit(solution)/shard_map/pallas_call | solution.py:388
  83.0 1.6 %copy.20 = bf16[256,256]{1,0:T(8,128)(2,1)} copy(bf16[256,256]{1,0:T(8,128)(2,1)} %get-tuple-element.10) | data formatting | bytes 262144
  84.6 1.5 %copy.21 = bf16[128,256]{1,0:T(8,128)(2,1)} copy(bf16[128,256]{1,0:T(8,128)(2,1)} %get-tuple-element.11) | data formatting | bytes 131072
  86.1 1.6 %copy.22 = bf16[256,256]{1,0:T(8,128)(2,1)} copy(bf16[256,256]{1,0:T(8,128)(2,1)} %get-tuple-element.12) | data formatting | bytes 262144
  87.6 1.5 %copy.23 = f32[27,4,256]{2,1,0:T(4,128)} copy(f32[27,4,256]{2,1,0:T(4,128)} %get-tuple-element.13) | data formatting | bytes 221184
  89.2 1.4 %copy.24 = f32[8,4,256]{2,1,0:T(4,128)} copy(f32[8,4,256]{2,1,0:T(4,128)} %get-tuple-element.14) | data formatting | bytes 65536

commit v2 on v1

--- a/solution.py
+++ b/solution.py
@@ -30,6 +30,10 @@
 
 def iota(shape, dim):
     return lax.broadcasted_iota(I32, shape, dim)
+
+
+def tap(k):
+    return slice(256 * k, 256 * k + 256)
 
 
 def slot_row(q, kind, half):
@@ -84,11 +88,12 @@
     dg_ref,
     w_ref,
     wd_ref,
+    wt,
     oht,
     picked,
+    pulled,
     cbo,
     total_ref,
-    acc,
     ext_grad,
     a1_src,
     a1_dst,
@@ -159,24 +164,17 @@
     feat = feat_ref[...]
     send_hot = onehot(iota((256, 128), 0) == send_ref[...])
     a1_src[...] = pack(mm_tn(send_hot, feat).astype(BF16), gdown_ref[...])
+    feat_t = feat.astype(F32).T.astype(BF16)
+    source = iota((384, 256), 0)
+    for k in range(TAPS):
+        oht[:, tap(k)] = onehot(source == nbr_ref[k : k + 1, :])
+    for k in range(TAPS):
+        picked[tap(k)] = mm(feat_t, oht[:256, tap(k)]).astype(BF16)
     pl.semaphore_wait(barrier, PEERS - 1)
     exchange(a1_src, a1_dst, 0)
-
-    feat_t = feat.astype(F32).T.astype(BF16)
-    acc[...] = jnp.zeros((256, 256), F32)
-    picked[TAPS] = jnp.zeros((256, 256), BF16)
-    oht[TAPS] = jnp.zeros((384, 256), BF16)
     w_copy.wait()
-
-    def local_tap(k, carry):
-        hot = onehot(iota((384, 256), 0) == nbr_ref[pl.ds(k, 1), :])
-        oht[k] = hot
-        own = mm(feat_t, hot[:256]).astype(BF16)
-        picked[k] = own
-        acc[...] += mm_tn(own, w_ref[k])
-        return carry
-
-    lax.fori_loop(0, TAPS, local_tap, 0)
+    for k in range(TAPS):
+        wt[:, tap(k)] = w_ref[k].T
     wd_copy.wait()
 
     exchange_wait(a1_src, a1_dst, 0)
@@ -241,12 +239,11 @@
         core_copy(g).start()
 
     def conv_group(g):
-        terms = []
-        for t in range(4):
-            k = 4 * g + t
-            whole = picked[k] + mm(halo_t, oht[k, 256:384]).astype(BF16)
-            terms.append(mm(whole, total_ref[...]))
-        give(g, terms)
+        taps = range(4 * g, min(4 * g + 4, TAPS))
+        for k in taps:
+            picked[tap(k)] += mm(halo_t, oht[256:, tap(k)]).astype(BF16)
+        terms = [mm(picked[tap(k)], total_ref[...]) for k in taps]
+        give(g, terms + [jnp.zeros((256, 256), F32)] * (4 - len(terms)))
 
     def add(g, xx, zs, other):
         here = part[core, g, xx, zs].astype(F32) + other.astype(F32)
@@ -293,21 +290,13 @@
             else:
                 dg_ref[4 * g - 28 : 4 * g - 24] = value
 
-    def forward(lo, hi):
-        def tap(k, carry):
-            rows = mm(halo_t, oht[k, 256:384]).astype(BF16)
-            acc[...] += mm_tn(rows, w_ref[k])
-            return carry
-
-        lax.fori_loop(lo, hi, tap, 0)
-
-    def backward(lo, hi):
-        def tap(k, carry):
-            pulled = mm_nt(total_ref[...], w_ref[k]).astype(BF16)
-            ext_grad[...] += mm(oht[k], pulled)
-            return carry
-
-        lax.fori_loop(lo, hi, tap, 0)
+    def pull(lo, hi):
+        for k in range(lo, hi):
+            pulled[tap(k)] = mm(total_ref[...], wt[:, tap(k)]).astype(BF16)
+
+    def scatter(lo, hi):
+        span = slice(256 * lo, 256 * hi)
+        return mm(oht[:, span], pulled[span])
 
     conv_group(0)
     conv_group(1)
@@ -329,15 +318,14 @@
     step1(5)
     step2(3)
     step3(2)
-    forward(0, 14)
+    summed_t = mm(wt[...], picked[...])
     step1(6)
     step2(4)
     step3(3)
     step4(0)
-    forward(14, 27)
-    conv_out = jnp.where(occupied, acc[...], 0.0).astype(BF16)
+    conv_out = jnp.where(occupied, summed_t.T, 0.0).astype(BF16)
     conv_ref[...] = conv_out
-    conv_t = conv_out.astype(F32).T.astype(BF16)
+    conv_t = conv_out.T
     give(7, [mm(conv_t, cbo[o]) for o in range(4)])
     step2(5)
     step3(4)
@@ -353,11 +341,12 @@
     step2(7)
     step3(6)
     step4(1)
-    ext_grad[...] = jnp.zeros((384, 256), F32)
-    backward(0, 14)
+    pull(0, 14)
+    ext_grad[...] = scatter(0, 14)
     step2(8)
     step3(7)
-    backward(14, 27)
+    pull(14, 27)
+    ext_grad[...] += scatter(14, 27)
     a2_src[...] = pack(coarse_part.astype(BF16), ext_grad[256:384].astype(BF16))
     exchange(a2_src, a2_dst, 1)
     step3(8)
@@ -381,11 +370,16 @@
             copy.wait_send()
 
 
+def place(*refs):
+    for held, out in zip(refs[:5], refs[5:]):
+        out[...] = held[...]
+
+
 def per_device(features, conv_weight, down_weight, grad_conv, grad_down, live_rows, halo_send, neighbors, coarse_code):
     vmem = pl.BlockSpec(memory_space=pltpu.VMEM)
     hbm = pl.BlockSpec(memory_space=pl.ANY)
     dma = pltpu.SemaphoreType.DMA
-    return pl.pallas_call(
+    results = pl.pallas_call(
         kernel,
         out_shape=(
             jax.ShapeDtypeStruct((256, 256), BF16),
@@ -399,11 +393,12 @@
         scratch_shapes=[
             pltpu.VMEM((27, 256, 256), BF16),
             pltpu.VMEM((8, 256, 256), BF16),
-            pltpu.VMEM((28, 384, 256), BF16),
-            pltpu.VMEM((28, 256, 256), BF16),
+            pltpu.VMEM((256, 256 * TAPS), BF16),
+            pltpu.VMEM((384, 256 * TAPS), BF16),
+            pltpu.VMEM((256 * TAPS, 256), BF16),
+            pltpu.VMEM((256 * TAPS, 256), BF16),
             pltpu.VMEM((8, 256, 256), BF16),
             pltpu.VMEM((256, 256), BF16),
-            pltpu.VMEM((256, 256), F32),
             pltpu.VMEM((384, 256), F32),
             pltpu.VMEM((PEERS, 8, 128), BF16),
             pltpu.VMEM((PEERS, 8, 128), BF16),
@@ -442,6 +437,12 @@
         neighbors,
         coarse_code.reshape(1, 256),
     )
+    return pl.pallas_call(
+        place,
+        out_shape=tuple(jax.ShapeDtypeStruct(r.shape, r.dtype) for r in results),
+        in_specs=[vmem] * 5,
+        out_specs=[vmem] * 5,
+    )(*results)
 
 
 def solution(mesh):

time: 91 us -> 64.9 us (0.71)
  Pallas kernels: 81.7 us -> 62.8 us
  local copies, waits for them, and re-layouts: 7.53 us -> 0 us
    pallas_call x1, Pallas kernels: 81.7 us -> 61 us  [per_device(): pl.pallas_call(kernel, out_shape=(jax.ShapeDtypeStruct((256, 256), BF16),...]
    unnamed x5 -> x0, local copies, waits for them, and re-layouts: 7.53 us -> none
    pallas_call x0 -> x1, Pallas kernels: none -> 1.83 us  [per_device(): pl.pallas_call(place, out_shape=tuple((jax.ShapeDtypeStruct(r.shape, r.dt...]
where the time goes in v2:
time: 64.9 us; the launch traced here: 64.1 us
  Pallas kernels  62.8 us (97%)
  between operations  1.29 us (2%)
    pallas_call x1, Pallas kernels, per_device(): pl.pallas_call(kernel, out_shape=(jax.ShapeDtypeStruct((256, 256), BF16),...  61 us
    pallas_call x1, Pallas kernels, per_device(): pl.pallas_call(place, out_shape=tuple((jax.ShapeDtypeStruct(r.shape, r.dt...  1.83 us

profile of v2, /device:TPU:16, one launch (start us, length us, event | category | flops | bytes accessed | tf_op | source)
XLA Modules:
  0.0 64.1 jit_solution(13156412759757660306)
XLA Ops:
  1.3 61.0 %shard_map.128 = (bf16[256,256]{1,0:T(8,128)(2,1)}, bf16[128,256]{1,0:T(8,128)(2,1)}, bf16[256,256]{1,0:T(8,128)(2,1)}, f32[27,4,256]{2,1,0:T(4,128)}, f32[8,4,256]{2,1,0:T(4,128)}) custom-call(bf16[256,256]{1,0:T(8,128)(2,1)} %feat_ref.1, bf16[27,256,256]{2,1,0:T(8,128)(2,1)} %w_hbm.1, bf16[8,256,256]{2,1,0:T(8,128)(2,1)} %wd_hbm.1, ...), custom_call_target="tpu_custom_call" | custom-call | flops 7000000000 | bytes 6000000 | tf_op jit(solution)/shard_map/pallas_call | solution.py:382
  62.3 1.8 %shard_map.129 = (bf16[256,256]{1,0:T(8,128)(2,1)}, bf16[128,256]{1,0:T(8,128)(2,1)}, bf16[256,256]{1,0:T(8,128)(2,1)}, f32[27,4,256]{2,1,0:T(4,128)}, f32[8,4,256]{2,1,0:T(4,128)}) custom-call(bf16[256,256]{1,0:T(8,128)(2,1)} %get-tuple-element.10.refs_0_, bf16[128,256]{1,0:T(8,128)(2,1)} %get-tuple-element.11.refs_1_, ...), custom_call_target="tpu_custom_call" | custom-call | tf_op jit(solution)/shard_map/pallas_call | solution.py:440

commit v3 on v2

v3 whole, which is shorter than its diff:
```python
import jax
import jax.numpy as jnp
from jax import lax
from jax.experimental import pallas as pl
from jax.experimental.pallas import tpu as pltpu
from jax.sharding import PartitionSpec as P

MESH = pl.DeviceIdType.MESH
BF16, F32, I32 = jnp.bfloat16, jnp.float32, jnp.int32
NX, NZ = 4, 8
TAPS, GROUPS = 27, 9
CHUNKS = ((0, 1), (1, 3), (3, 5), (5, 7), (7, 9))
PARTS = len(CHUNKS)


def mm(a, b):
    return jnp.dot(a, b, preferred_element_type=F32)


def mm_nt(a, b):
    return lax.dot_general(a, b, (((1,), (1,)), ((), ())), preferred_element_type=F32)


def mm_tn(a, b):
    return lax.dot_general(a, b, (((0,), (0,)), ((), ())), preferred_element_type=F32)


def onehot(mask):
    return jnp.where(mask, 1.0, 0.0).astype(BF16)


def iota(shape, dim):
    return lax.broadcasted_iota(I32, shape, dim)


def tap(k):
    return slice(256 * k, 256 * k + 256)


def slot_row(q, kind, half, arriving):
    peer = q // 2
    line, column = (peer // 2) % NZ, 2 * (peer // 16) + peer % 2
    slot = 8 * column + line if arriving else 8 * line + column
    return 8 * slot + 2 * (2 * kind + q % 2) + half


def pack(first, second):
    row, q = iota((512, 128), 0), iota((512, 128), 1)
    total = jnp.zeros((512, 128), F32)
    for kind, rows in ((0, first), (1, second)):
        for half in range(2):
            place = onehot(row == slot_row(q, kind, half, False))
            total += mm(place, rows[:, half * 128 : half * 128 + 128])
    return total.reshape(8, 8, 8, 128).astype(BF16)


def unpack(slots, kind):
    q, row = iota((128, 512), 0), iota((128, 512), 1)
    flat = slots.astype(F32).reshape(512, 128).astype(BF16)
    return jnp.concatenate(
        [mm(onehot(row == slot_row(q, kind, half, True)), flat) for half in range(2)], axis=1
    )


def interleave(terms):
    a = [term.reshape(32, 8, 256) for term in terms]
    r = [pltpu.roll(value, 4, 1) for value in a]
    low = iota((32, 8, 256), 1) < 4
    first = jnp.concatenate(
        [jnp.where(low, a[0], r[1]), jnp.where(low, a[2], r[3])], axis=1
    )
    second = jnp.concatenate(
        [jnp.where(low, r[0], a[1]), jnp.where(low, r[2], a[3])], axis=1
    )
    return first, second


def kernel(
    feat_ref,
    w_hbm,
    wd_hbm,
    gconv_ref,
    gdown_ref,
    live_ref,
    send_ref,
    nbr_ref,
    code_ref,
    conv_ref,
    down_ref,
    gfeat_ref,
    wg_ref,
    dg_ref,
    w_ref,
    wd_ref,
    wt,
    oht,
    picked,
    pulled,
    cbo,
    total_ref,
    ext_grad,
    a1_src,
    a1_mid,
    a1_dst,
    a2_src,
    a2_mid,
    a2_dst,
    mine,
    give0,
    got0,
    give1,
    got1,
    give2,
    got2,
    give3,
    got3,
    w_sem,
    a_ss,
    a_rs,
    r_ss,
    r_rs,
    z_ss,
    z_rs,
):
    me = lax.axis_index("space")
    x, z, core = me // 16, (me // 2) % NZ, me % 2
    x1, x2, x3 = x + 1 - 2 * (x % 2), (x + 2) % NX, 3 - x

    column = 2 * x + core

    def device(xx, zz, cc):
        return {"space": (xx * NZ + zz) * 2 + cc}

    def in_line(i):
        return (z + i) % NZ

    def in_plane(i):
        return (column + i) % 8

    barrier = pltpu.get_barrier_semaphore()
    for i in range(1, 8):
        for to in (device(x, in_line(i), core), device(in_plane(i) // 2, z, in_plane(i) % 2)):
            pl.semaphore_signal(barrier, inc=1, device_id=to, device_id_type=MESH)
    w_copy = pltpu.make_async_copy(w_hbm, w_ref, w_sem.at[0])
    wd_copy = pltpu.make_async_copy(wd_hbm, wd_ref, w_sem.at[1])
    w_copy.start()
    wd_copy.start()

    def remote(src, dst, ss, rs, to):
        return pltpu.make_async_remote_copy(
            src_ref=src, dst_ref=dst, send_sem=ss, recv_sem=rs, device_id=to, device_id_type=MESH
        )

    def line_start(src, mid, which):
        ss, rs = a_ss.at[which, 0], a_rs.at[which, 0]
        for i in range(1, 8):
            to = in_line(i)
            remote(src.at[to], mid.at[z], ss, rs, device(x, to, core)).start()
        pltpu.make_async_copy(src.at[z], mid.at[z], rs).start()

    def line_wait(src, mid, which):
        pltpu.make_async_copy(src, mid, a_rs.at[which, 0]).wait()

    def plane_start(mid, dst, which):
        ss, rs = a_ss.at[which, 1], a_rs.at[which, 1]
        for i in range(1, 8):
            to = in_plane(i)
            remote(mid.at[:, to], dst.at[column], ss, rs, device(to // 2, z, to % 2)).start()
        pltpu.make_async_copy(mid.at[:, column], dst.at[column], rs).start()

    def plane_wait(mid, dst, which):
        pltpu.make_async_copy(mid, dst, a_rs.at[which, 1]).wait()

    def exchange_sent(buffer, which):
        rest = buffer.at[pl.ds(0, 7)]
        for phase in range(2):
            pltpu.make_async_copy(rest, rest, a_ss.at[which, phase]).wait()

    feat = feat_ref[...]
    send_hot = onehot(iota((256, 128), 0) == send_ref[...])
    a1_src[...] = pack(mm_tn(send_hot, feat).astype(BF16), gdown_ref[...])
    pl.semaphore_wait(barrier, 14)
    line_start(a1_src, a1_mid, 0)
    feat_t = feat.astype(F32).T.astype(BF16)
    source = iota((384, 256), 0)
    for k in range(TAPS):
        oht[:, tap(k)] = onehot(source == nbr_ref[k : k + 1, :])
    line_wait(a1_src, a1_mid, 0)
    plane_start(a1_mid, a1_dst, 0)
    for k in range(TAPS):
        picked[tap(k)] = mm(feat_t, oht[:256, tap(k)]).astype(BF16)
    w_copy.wait()
    for k in range(TAPS):
        wt[:, tap(k)] = w_ref[k].T
    wd_copy.wait()

    plane_wait(a1_mid, a1_dst, 0)
    arrived = a1_dst[...]
    halo_t = unpack(arrived, 0).T.astype(BF16)
    coarse_back = unpack(arrived, 1).astype(BF16)
    code_row = code_ref[...]
    code_col = jnp.broadcast_to(code_row.astype(F32), (8, 256)).T[:, :1].astype(I32)
    from_down = jnp.zeros((256, 256), F32)
    for o in range(8):
        rows = mm(onehot(code_col == 8 * iota((256, 128), 1) + o), coarse_back).astype(BF16)
        cbo[o] = rows
        from_down += mm_nt(rows, wd_ref[o])
    occupied = iota((256, 256), 0) < live_ref[0]
    total = jnp.where(occupied, gconv_ref[...].astype(F32) + from_down, 0.0).astype(BF16)
    total_ref[...] = total

    near, far = (x1, x3), (x3, x1)

    def span(c):
        return pl.ds(CHUNKS[c][0], CHUNKS[c][1] - CHUNKS[c][0])

    def copies(c, step):
        s = span(c)
        if step == 0:
            return [remote(give0.at[s], got0.at[s], r_ss.at[c, 0, 0], r_rs.at[c, 0, 0], device(x, z, 1 - core))]
        if step == 3:
            return [
                remote(give3.at[in_line(i), s], got3.at[z, s], z_ss.at[c, i], z_rs.at[c, i], device(x, in_line(i), core))
                for i in range(1, NZ)
            ]
        give, got, to = (give1, got1, near) if step == 1 else (give2, got2, far)
        return [
            remote(give.at[h, s], got.at[h, s], r_ss.at[c, step, h], r_rs.at[c, step, h], device(to[h], z, core))
            for h in range(2)
        ]

    def send(c, step):
        for copy in copies(c, step):
            copy.start()

    def receive(c, step):
        for copy in copies(c, step):
            copy.wait_recv()

    def give(g, terms):
        first, second = interleave(terms)
        own = jnp.where(core == 0, first, second)
        other = jnp.where(core == 0, second, first).astype(BF16)
        for h in range(2):
            half = slice(128 * h, 128 * h + 128)
            mine[g, h] = own[:, :, half].reshape(NX, NZ, 16, 128)
            give0[g, h] = other[:, :, half].reshape(NX, NZ, 16, 128)

    def step1(c):
        s = span(c)
        receive(c, 0)
        for h in range(2):
            for i, xx in enumerate((near[h], x2)):
                give1[h, s, i] = (mine[s, h, xx] + got0[s, h, xx].astype(F32)).astype(BF16)
        send(c, 1)
        for h in range(2):
            for xx in (x, far[h]):
                mine[s, h, xx] += got0[s, h, xx].astype(F32)

    def step2(c):
        s = span(c)
        receive(c, 1)
        for h in range(2):
            give2[h, s] = (mine[s, h, far[h]] + got1[h, s, 1].astype(F32)).astype(BF16)
        send(c, 2)
        for h in range(2):
            mine[s, h, x] += got1[h, s, 0].astype(F32)

    def step3(c):
        s = span(c)
        receive(c, 2)
        for h in range(2):
            value = mine[s, h, x] + got2[h, s].astype(F32)
            mine[s, h, x] = value
            for zz in range(NZ):
                give3[zz, s, :, 128 * h : 128 * h + 128] = value[:, zz].astype(BF16)
        send(c, 3)

    def final(c):
        receive(c, 3)
        for g in range(*CHUNKS[c]):
            value = jnp.concatenate([mine[g, h, x, z] for h in range(2)], axis=1)
            for i in range(1, NZ):
                value += got3[in_line(i), g].astype(F32)
            value = (value * (1.0 / 64.0)).reshape(4, 4, 256)
            if g < 6:
                wg_ref[4 * g : 4 * g + 4] = value
            elif g == 6:
                wg_ref[24:27] = value[:3]
            else:
                dg_ref[4 * g - 28 : 4 * g - 24] = value

    def conv_group(g):
        taps = range(4 * g, min(4 * g + 4, TAPS))
        for k in taps:
            picked[tap(k)] += mm(halo_t, oht[256:, tap(k)]).astype(BF16)
        terms = [mm(picked[tap(k)], total_ref[...]) for k in taps]
        give(g, terms + [jnp.zeros((256, 256), F32)] * (4 - len(terms)))

    def pull(lo, hi):
        for k in range(lo, hi):
            pulled[tap(k)] = mm(total_ref[...], wt[:, tap(k)]).astype(BF16)

    def scatter(lo, hi):
        span = slice(256 * lo, 256 * hi)
        return mm(oht[:, span], pulled[span])

    for c in range(4):
        for g in range(*CHUNKS[c]):
            conv_group(g)
        send(c, 0)
        if c > 0:
            step1(c - 1)
    summed_t = mm(wt[...], picked[...])
    step1(3)
    conv_out = jnp.where(occupied, summed_t.T, 0.0).astype(BF16)
    conv_ref[...] = conv_out
    conv_t = conv_out.T
    give(7, [mm(conv_t, cbo[o]) for o in range(4)])
    give(8, [mm(conv_t, cbo[o]) for o in range(4, 8)])
    send(4, 0)
    step2(0)
    coarse_part = jnp.zeros((128, 256), F32)
    for o in range(8):
        hot = onehot(code_row == 8 * iota((128, 256), 0) + o)
        coarse_part += mm(mm(hot, conv_out).astype(BF16), wd_ref[o])
    step1(4)
    pull(0, 27)
    step2(1)
    ext_grad[...] = scatter(0, 27)
    a2_src[...] = pack(coarse_part.astype(BF16), ext_grad[256:384].astype(BF16))
    line_start(a2_src, a2_mid, 1)
    step3(0)
    step2(2)
    step3(1)
    line_wait(a2_src, a2_mid, 1)
    plane_start(a2_mid, a2_dst, 1)
    step2(3)
    step3(2)
    final(0)
    step2(4)
    step3(3)
    final(1)
    step3(4)
    plane_wait(a2_mid, a2_dst, 1)
    arrived = a2_dst[...]
    down_ref[...] = unpack(arrived, 0).astype(BF16)
    returned = unpack(arrived, 1).astype(BF16)
    gfeat_ref[...] = (ext_grad[:256] + mm(send_hot, returned)).astype(BF16)
    final(2)
    final(3)
    final(4)
    exchange_sent(a1_src, 0)
    exchange_sent(a2_src, 1)
    for c in range(PARTS):
        for step in range(4):
            for copy in copies(c, step):
                copy.wait_send()


def place(*refs):
    for held, out in zip(refs[:5], refs[5:]):
        out[...] = held[...]


def per_device(features, conv_weight, down_weight, grad_conv, grad_down, live_rows, halo_send, neighbors, coarse_code):
    vmem = pl.BlockSpec(memory_space=pltpu.VMEM)
    hbm = pl.BlockSpec(memory_space=pl.ANY)
    dma = pltpu.SemaphoreType.DMA
    results = pl.pallas_call(
        kernel,
        out_shape=(
            jax.ShapeDtypeStruct((256, 256), BF16),
            jax.ShapeDtypeStruct((128, 256), BF16),
            jax.ShapeDtypeStruct((256, 256), BF16),
            jax.ShapeDtypeStruct((27, 4, 256), F32),
            jax.ShapeDtypeStruct((8, 4, 256), F32),
        ),
        in_specs=[vmem, hbm, hbm, vmem, vmem, pl.BlockSpec(memory_space=pltpu.SMEM), vmem, vmem, vmem],
        out_specs=[vmem] * 5,
        scratch_shapes=[
            pltpu.VMEM((27, 256, 256), BF16),
            pltpu.VMEM((8, 256, 256), BF16),
            pltpu.VMEM((256, 256 * TAPS), BF16),
            pltpu.VMEM((384, 256 * TAPS), BF16),
            pltpu.VMEM((256 * TAPS, 256), BF16),
            pltpu.VMEM((256 * TAPS, 256), BF16),
            pltpu.VMEM((8, 256, 256), BF16),
            pltpu.VMEM((256, 256), BF16),
            pltpu.VMEM((384, 256), F32),
            *[pltpu.VMEM((8, 8, 8, 128), BF16)] * 6,
            pltpu.VMEM((GROUPS, 2, NX, NZ, 16, 128), F32),
            *[pltpu.VMEM((GROUPS, 2, NX, NZ, 16, 128), BF16)] * 2,
            *[pltpu.VMEM((2, GROUPS, 2, NZ, 16, 128), BF16)] * 2,
            *[pltpu.VMEM((2, GROUPS, NZ, 16, 128), BF16)] * 2,
            *[pltpu.VMEM((NZ, GROUPS, 16, 256), BF16)] * 2,
            dma((2,)),
            dma((2, 2)),
            dma((2, 2)),
            dma((PARTS, 3, 2)),
            dma((PARTS, 3, 2)),
            dma((PARTS, NZ)),
            dma((PARTS, NZ)),
        ],
        compiler_params=pltpu.CompilerParams(
            collective_id=0, has_side_effects=True, vmem_limit_bytes=56 * 2**20
        ),
        cost_estimate=pl.CostEstimate(flops=7 * 10**9, bytes_accessed=6 * 10**6, transcendentals=0),
    )(
        features,
        conv_weight,
        down_weight,
        grad_conv,
        grad_down,
        live_rows,
        halo_send,
        neighbors,
        coarse_code.reshape(1, 256),
    )
    return pl.pallas_call(
        place,
        out_shape=tuple(jax.ShapeDtypeStruct(r.shape, r.dtype) for r in results),
        in_specs=[vmem] * 5,
        out_specs=[vmem] * 5,
    )(*results)


def solution(mesh):
    rows = P(("dp", "space"), None)
    return jax.shard_map(
        per_device,
        mesh=mesh,
        in_specs=(rows, P(), P(), rows, rows, P(("dp", "space")), rows, P(None, ("dp", "space")), P(("dp", "space"))),
        out_specs=(rows, rows, rows, P("dp", "space", None), P("dp", "space", None)),
        check_vma=False,
    )
```

time: 64.9 us -> 59.2 us (0.912)
  Pallas kernels: 62.8 us -> 57.5 us
    pallas_call x1, Pallas kernels: 61 us -> 55.7 us  [per_device(): pl.pallas_call(kernel, out_shape=(jax.ShapeDtypeStruct((256, 256), BF16),...]
where the time goes in v3:
time: 59.2 us; the launch traced here: 58.8 us
  Pallas kernels  57.5 us (97%)
  between operations  1.29 us (2%)
    pallas_call x1, Pallas kernels, per_device(): pl.pallas_call(kernel, out_shape=(jax.ShapeDtypeStruct((256, 256), BF16),...  55.7 us
    pallas_call x1, Pallas kernels, per_device(): pl.pallas_call(place, out_shape=tuple((jax.ShapeDtypeStruct(r.shape, r.dt...  1.83 us

profile of v3, /device:TPU:16, one launch (start us, length us, event | category | flops | bytes accessed | tf_op | source)
XLA Modules:
  0.0 58.8 jit_solution(16683735734690534316)
XLA Ops:
  1.3 55.7 %shard_map.128 = (bf16[256,256]{1,0:T(8,128)(2,1)}, bf16[128,256]{1,0:T(8,128)(2,1)}, bf16[256,256]{1,0:T(8,128)(2,1)}, f32[27,4,256]{2,1,0:T(4,128)}, f32[8,4,256]{2,1,0:T(4,128)}) custom-call(bf16[256,256]{1,0:T(8,128)(2,1)} %feat_ref.1, bf16[27,256,256]{2,1,0:T(8,128)(2,1)} %w_hbm.1, bf16[8,256,256]{2,1,0:T(8,128)(2,1)} %wd_hbm.1, ...), custom_call_target="tpu_custom_call" | custom-call | flops 7000000000 | bytes 6000000 | tf_op jit(solution)/shard_map/pallas_call | solution.py:370
  56.9 1.8 %shard_map.129 = (bf16[256,256]{1,0:T(8,128)(2,1)}, bf16[128,256]{1,0:T(8,128)(2,1)}, bf16[256,256]{1,0:T(8,128)(2,1)}, f32[27,4,256]{2,1,0:T(4,128)}, f32[8,4,256]{2,1,0:T(4,128)}) custom-call(bf16[256,256]{1,0:T(8,128)(2,1)} %get-tuple-element.10.refs_0_, bf16[128,256]{1,0:T(8,128)(2,1)} %get-tuple-element.11.refs_1_, ...), custom_call_target="tpu_custom_call" | custom-call | tf_op jit(solution)/shard_map/pallas_call | solution.py:420

commit v4 on v3

--- a/solution.py
+++ b/solution.py
@@ -333,12 +333,12 @@
     step3(0)
     step2(2)
     step3(1)
-    line_wait(a2_src, a2_mid, 1)
-    plane_start(a2_mid, a2_dst, 1)
     step2(3)
     step3(2)
     final(0)
     step2(4)
+    line_wait(a2_src, a2_mid, 1)
+    plane_start(a2_mid, a2_dst, 1)
     step3(3)
     final(1)
     step3(4)

time: 59.2 us -> 59 us (level)
  no operation moved by 1% of the time
where the time goes in v4:
time: 59 us; the launch traced here: 58.8 us
  Pallas kernels  57.5 us (97%)
  between operations  1.29 us (2%)
    pallas_call x1, Pallas kernels, per_device(): pl.pallas_call(kernel, out_shape=(jax.ShapeDtypeStruct((256, 256), BF16),...  55.7 us
    pallas_call x1, Pallas kernels, per_device(): pl.pallas_call(place, out_shape=tuple((jax.ShapeDtypeStruct(r.shape, r.dt...  1.83 us

profile of v4, /device:TPU:16, one launch (start us, length us, event | category | flops | bytes accessed | tf_op | source)
XLA Modules:
  0.0 58.8 jit_solution(2090254847473900288)
XLA Ops:
  1.3 55.7 %shard_map.128 = (bf16[256,256]{1,0:T(8,128)(2,1)}, bf16[128,256]{1,0:T(8,128)(2,1)}, bf16[256,256]{1,0:T(8,128)(2,1)}, f32[27,4,256]{2,1,0:T(4,128)}, f32[8,4,256]{2,1,0:T(4,128)}) custom-call(bf16[256,256]{1,0:T(8,128)(2,1)} %feat_ref.1, bf16[27,256,256]{2,1,0:T(8,128)(2,1)} %w_hbm.1, bf16[8,256,256]{2,1,0:T(8,128)(2,1)} %wd_hbm.1, ...), custom_call_target="tpu_custom_call" | custom-call | flops 7000000000 | bytes 6000000 | tf_op jit(solution)/shard_map/pallas_call | solution.py:370
  57.0 1.8 %shard_map.129 = (bf16[256,256]{1,0:T(8,128)(2,1)}, bf16[128,256]{1,0:T(8,128)(2,1)}, bf16[256,256]{1,0:T(8,128)(2,1)}, f32[27,4,256]{2,1,0:T(4,128)}, f32[8,4,256]{2,1,0:T(4,128)}) custom-call(bf16[256,256]{1,0:T(8,128)(2,1)} %get-tuple-element.10.refs_0_, bf16[128,256]{1,0:T(8,128)(2,1)} %get-tuple-element.11.refs_1_, ...), custom_call_target="tpu_custom_call" | custom-call | tf_op jit(solution)/shard_map/pallas_call | solution.py:420

commit v5 on v4

--- a/solution.py
+++ b/solution.py
@@ -76,20 +76,27 @@
 
 
 def kernel(
-    feat_ref,
+    feat_hbm,
     w_hbm,
     wd_hbm,
+    gconv_hbm,
+    gdown_hbm,
+    live_ref,
+    send_ref,
+    nbr_hbm,
+    code_ref,
+    conv_hbm,
+    down_hbm,
+    gfeat_hbm,
+    wg_ref,
+    dg_ref,
+    feat_ref,
     gconv_ref,
     gdown_ref,
-    live_ref,
-    send_ref,
     nbr_ref,
-    code_ref,
     conv_ref,
     down_ref,
     gfeat_ref,
-    wg_ref,
-    dg_ref,
     w_ref,
     wd_ref,
     wt,
@@ -115,6 +122,7 @@
     give3,
     got3,
     w_sem,
+    io_sem,
     a_ss,
     a_rs,
     r_ss,
@@ -141,6 +149,18 @@
     for i in range(1, 8):
         for to in (device(x, in_line(i), core), device(in_plane(i) // 2, z, in_plane(i) % 2)):
             pl.semaphore_signal(barrier, inc=1, device_id=to, device_id_type=MESH)
+    loads = [
+        pltpu.make_async_copy(held, ref, io_sem.at[i])
+        for i, (held, ref) in enumerate(
+            ((feat_hbm, feat_ref), (gdown_hbm, gdown_ref), (nbr_hbm, nbr_ref), (gconv_hbm, gconv_ref))
+        )
+    ]
+    for load in loads:
+        load.start()
+    stores = [
+        pltpu.make_async_copy(ref, held, io_sem.at[4 + i])
+        for i, (ref, held) in enumerate(((conv_ref, conv_hbm), (down_ref, down_hbm), (gfeat_ref, gfeat_hbm)))
+    ]
     w_copy = pltpu.make_async_copy(w_hbm, w_ref, w_sem.at[0])
     wd_copy = pltpu.make_async_copy(wd_hbm, wd_ref, w_sem.at[1])
     w_copy.start()
@@ -176,6 +196,8 @@
         for phase in range(2):
             pltpu.make_async_copy(rest, rest, a_ss.at[which, phase]).wait()
 
+    loads[0].wait()
+    loads[1].wait()
     feat = feat_ref[...]
     send_hot = onehot(iota((256, 128), 0) == send_ref[...])
     a1_src[...] = pack(mm_tn(send_hot, feat).astype(BF16), gdown_ref[...])
@@ -183,6 +205,7 @@
     line_start(a1_src, a1_mid, 0)
     feat_t = feat.astype(F32).T.astype(BF16)
     source = iota((384, 256), 0)
+    loads[2].wait()
     for k in range(TAPS):
         oht[:, tap(k)] = onehot(source == nbr_ref[k : k + 1, :])
     line_wait(a1_src, a1_mid, 0)
@@ -193,6 +216,7 @@
     for k in range(TAPS):
         wt[:, tap(k)] = w_ref[k].T
     wd_copy.wait()
+    loads[3].wait()
 
     plane_wait(a1_mid, a1_dst, 0)
     arrived = a1_dst[...]
@@ -315,6 +339,7 @@
     step1(3)
     conv_out = jnp.where(occupied, summed_t.T, 0.0).astype(BF16)
     conv_ref[...] = conv_out
+    stores[0].start()
     conv_t = conv_out.T
     give(7, [mm(conv_t, cbo[o]) for o in range(4)])
     give(8, [mm(conv_t, cbo[o]) for o in range(4, 8)])
@@ -345,11 +370,15 @@
     plane_wait(a2_mid, a2_dst, 1)
     arrived = a2_dst[...]
     down_ref[...] = unpack(arrived, 0).astype(BF16)
+    stores[1].start()
     returned = unpack(arrived, 1).astype(BF16)
     gfeat_ref[...] = (ext_grad[:256] + mm(send_hot, returned)).astype(BF16)
+    stores[2].start()
     final(2)
     final(3)
     final(4)
+    for store in stores:
+        store.wait()
     exchange_sent(a1_src, 0)
     exchange_sent(a2_src, 1)
     for c in range(PARTS):
@@ -376,9 +405,16 @@
             jax.ShapeDtypeStruct((27, 4, 256), F32),
             jax.ShapeDtypeStruct((8, 4, 256), F32),
         ),
-        in_specs=[vmem, hbm, hbm, vmem, vmem, pl.BlockSpec(memory_space=pltpu.SMEM), vmem, vmem, vmem],
-        out_specs=[vmem] * 5,
+        in_specs=[hbm, hbm, hbm, hbm, hbm, pl.BlockSpec(memory_space=pltpu.SMEM), vmem, hbm, vmem],
+        out_specs=[hbm, hbm, hbm, vmem, vmem],
         scratch_shapes=[
+            pltpu.VMEM((256, 256), BF16),
+            pltpu.VMEM((256, 256), BF16),
+            pltpu.VMEM((128, 256), BF16),
+            pltpu.VMEM((27, 256), I32),
+            pltpu.VMEM((256, 256), BF16),
+            pltpu.VMEM((128, 256), BF16),
+            pltpu.VMEM((256, 256), BF16),
             pltpu.VMEM((27, 256, 256), BF16),
             pltpu.VMEM((8, 256, 256), BF16),
             pltpu.VMEM((256, 256 * TAPS), BF16),
@@ -395,6 +431,7 @@
             *[pltpu.VMEM((2, GROUPS, NZ, 16, 128), BF16)] * 2,
             *[pltpu.VMEM((NZ, GROUPS, 16, 256), BF16)] * 2,
             dma((2,)),
+            dma((7,)),
             dma((2, 2)),
             dma((2, 2)),
             dma((PARTS, 3, 2)),

time: 59 us -> 58.7 us (level)
  no operation moved by 1% of the time
where the time goes in v5:
time: 58.7 us; the launch traced here: 58.5 us
  Pallas kernels  57.2 us (97%)
  between operations  1.29 us (2%)
    pallas_call x1, Pallas kernels, per_device(): pl.pallas_call(kernel, out_shape=(jax.ShapeDtypeStruct((256, 256), BF16),...  55.3 us
    pallas_call x1, Pallas kernels, per_device(): pl.pallas_call(place, out_shape=tuple((jax.ShapeDtypeStruct(r.shape, r.dt...  1.83 us

profile of v5, /device:TPU:16, one launch (start us, length us, event | category | flops | bytes accessed | tf_op | source)
XLA Modules:
  0.0 58.5 jit_solution(8257739344583016063)
XLA Ops:
  1.3 55.3 %shard_map.128 = (bf16[256,256]{1,0:T(8,128)(2,1)}, bf16[128,256]{1,0:T(8,128)(2,1)}, bf16[256,256]{1,0:T(8,128)(2,1)}, f32[27,4,256]{2,1,0:T(4,128)}, f32[8,4,256]{2,1,0:T(4,128)}) custom-call(bf16[256,256]{1,0:T(8,128)(2,1)} %feat_hbm.1, bf16[27,256,256]{2,1,0:T(8,128)(2,1)} %w_hbm.1, bf16[8,256,256]{2,1,0:T(8,128)(2,1)} %wd_hbm.1, ...), custom_call_target="tpu_custom_call" | custom-call | flops 7000000000 | bytes 6000000 | tf_op jit(solution)/shard_map/pallas_call | solution.py:399
  56.6 1.8 %shard_map.129 = (bf16[256,256]{1,0:T(8,128)(2,1)}, bf16[128,256]{1,0:T(8,128)(2,1)}, bf16[256,256]{1,0:T(8,128)(2,1)}, f32[27,4,256]{2,1,0:T(4,128)}, f32[8,4,256]{2,1,0:T(4,128)}) custom-call(bf16[256,256]{1,0:T(8,128)(2,1)} %get-tuple-element.10.refs_0_, bf16[128,256]{1,0:T(8,128)(2,1)} %get-tuple-element.11.refs_1_, ...), custom_call_target="tpu_custom_call" | custom-call | tf_op jit(solution)/shard_map/pallas_call | solution.py:457

commit v6 on v5

--- a/solution.py
+++ b/solution.py
@@ -146,7 +146,7 @@
         return (column + i) % 8
 
     barrier = pltpu.get_barrier_semaphore()
-    for i in range(1, 8):
+    for i in (4, 3, 5, 2, 6, 1, 7):
         for to in (device(x, in_line(i), core), device(in_plane(i) // 2, z, in_plane(i) % 2)):
             pl.semaphore_signal(barrier, inc=1, device_id=to, device_id_type=MESH)
     loads = [
@@ -173,7 +173,7 @@
 
     def line_start(src, mid, which):
         ss, rs = a_ss.at[which, 0], a_rs.at[which, 0]
-        for i in range(1, 8):
+        for i in (4, 3, 5, 2, 6, 1, 7):
             to = in_line(i)
             remote(src.at[to], mid.at[z], ss, rs, device(x, to, core)).start()
         pltpu.make_async_copy(src.at[z], mid.at[z], rs).start()
@@ -183,7 +183,7 @@
 
     def plane_start(mid, dst, which):
         ss, rs = a_ss.at[which, 1], a_rs.at[which, 1]
-        for i in range(1, 8):
+        for i in (4, 3, 5, 2, 6, 1, 7):
             to = in_plane(i)
             remote(mid.at[:, to], dst.at[column], ss, rs, device(to // 2, z, to % 2)).start()
         pltpu.make_async_copy(mid.at[:, column], dst.at[column], rs).start()

time: 58.7 us -> 58 us (0.988)
  Pallas kernels: 57.2 us -> 56.6 us
where the time goes in v6:
time: 58 us; the launch traced here: 57.9 us
  Pallas kernels  56.6 us (98%)
  between operations  1.29 us (2%)
    pallas_call x1, Pallas kernels, per_device(): pl.pallas_call(kernel, out_shape=(jax.ShapeDtypeStruct((256, 256), BF16),...  54.8 us
    pallas_call x1, Pallas kernels, per_device(): pl.pallas_call(place, out_shape=tuple((jax.ShapeDtypeStruct(r.shape, r.dt...  1.83 us

profile of v6, /device:TPU:16, one launch (start us, length us, event | category | flops | bytes accessed | tf_op | source)
XLA Modules:
  0.0 57.9 jit_solution(756036749746911858)
XLA Ops:
  1.3 54.8 %shard_map.128 = (bf16[256,256]{1,0:T(8,128)(2,1)}, bf16[128,256]{1,0:T(8,128)(2,1)}, bf16[256,256]{1,0:T(8,128)(2,1)}, f32[27,4,256]{2,1,0:T(4,128)}, f32[8,4,256]{2,1,0:T(4,128)}) custom-call(bf16[256,256]{1,0:T(8,128)(2,1)} %feat_hbm.1, bf16[27,256,256]{2,1,0:T(8,128)(2,1)} %w_hbm.1, bf16[8,256,256]{2,1,0:T(8,128)(2,1)} %wd_hbm.1, ...), custom_call_target="tpu_custom_call" | custom-call | flops 7000000000 | bytes 6000000 | tf_op jit(solution)/shard_map/pallas_call | solution.py:399
  56.1 1.8 %shard_map.129 = (bf16[256,256]{1,0:T(8,128)(2,1)}, bf16[128,256]{1,0:T(8,128)(2,1)}, bf16[256,256]{1,0:T(8,128)(2,1)}, f32[27,4,256]{2,1,0:T(4,128)}, f32[8,4,256]{2,1,0:T(4,128)}) custom-call(bf16[256,256]{1,0:T(8,128)(2,1)} %get-tuple-element.10.refs_0_, bf16[128,256]{1,0:T(8,128)(2,1)} %get-tuple-element.11.refs_1_, ...), custom_call_target="tpu_custom_call" | custom-call | tf_op jit(solution)/shard_map/pallas_call | solution.py:457
